TPU v7x, 512 devices: a whole 4x4x16 slice. The times are simulated.
512 devices in a mesh: row: 64 (over y, z_hi, x, core), col: 8 (over z_lo).
Axes of the slice: x: 4, y: 4, z: 16 (z_hi: 2, z_lo: 8; z = z_hi * 8 + z_lo), core: 2. Of those that a mesh axis runs over, the one named last changes fastest.
Arguments:
- queries: bfloat16 [8192, 8192], P('row'), may hold values from -18 to 18
- keys: bfloat16 [8192, 512], P(('row', 'col')), may hold values from -18 to 18
- values: bfloat16 [8192, 512], P(('row', 'col')), may hold values from -6 to 6
- order: int32 [8192], P(('row', 'col')), may hold values from 0 to 8191, as said below
Outputs:
- attended: bfloat16 [8192, 8192], P(('row', 'col'))
Inputs may be any that keep to these rules, and one draw needn't show every extreme that they name: `order`: each device's 16 entries are consecutive increasing positions; every position of the sequence appears once.
All inputs are finite; a program needn't handle non-finite values.
Results may differ from a plain program's by a relative error of at most 0.03.
Values may be sent and summed in bfloat16 or wider, within the bound.
A program may use at most 64 MiB of HBM per device.

v0:
```python
import jax
import jax.numpy as jnp
from jax import lax
from jax.sharding import PartitionSpec as P

HD = 128
KVH = 4
GROUP = 16


def shards(queries, keys, values, order):
    row_count = lax.axis_size("row")
    col_count = lax.axis_size("col")
    row_here = lax.axis_index("row")
    col_here = lax.axis_index("col")
    local_rows = order.shape[0]
    score_scale = HD ** (-0.5)
    every_pos = lax.all_gather(order, ("row", "col"), axis=0, tiled=True)
    position_grid = every_pos.reshape(row_count, col_count, local_rows)
    query_pos = lax.dynamic_index_in_dim(position_grid, row_here, 0, keepdims=False).reshape(-1)
    key_pos = lax.dynamic_index_in_dim(position_grid, col_here, 1, keepdims=False).reshape(-1)
    query_count = queries.shape[0]
    grouped = queries.reshape(query_count, KVH, GROUP, HD)

    def update(state, block):
        running_max, running_sum, accumulated = state
        key_block, value_block, block_pos = block
        scores = (
            jnp.einsum("qgrd,kgd->grqk", grouped, key_block, preferred_element_type=jnp.float32)
            * score_scale
        )
        visible = block_pos[None, :] <= query_pos[:, None]
        scores = jnp.where(visible, scores, -1e30)
        new_max = jnp.maximum(running_max, scores.max(-1))
        raised = jnp.where(visible, jnp.exp(scores - new_max[..., None]), 0.0)
        rescale = jnp.exp(running_max - new_max)
        new_sum = running_sum * rescale + raised.sum(-1)
        product = jnp.einsum(
            "grqk,kgd->qgrd",
            raised.astype(jnp.bfloat16),
            value_block,
            preferred_element_type=jnp.float32,
        )
        new_acc = accumulated * jnp.transpose(rescale, (2, 0, 1))[..., None] + product
        return ((new_max, new_sum, new_acc), None)

    start_state = (
        jnp.full((KVH, GROUP, query_count), -1e30, jnp.float32),
        jnp.zeros((KVH, GROUP, query_count), jnp.float32),
        jnp.zeros((query_count, KVH, GROUP, HD), jnp.float32),
    )
    key_piece = lax.all_gather(keys, "row", axis=0, tiled=True)
    value_piece = lax.all_gather(values, "row", axis=0, tiled=True)
    count_rows = key_piece.shape[0]
    block_size = 128
    block_count = count_rows // block_size
    blocks = (
        key_piece.reshape(block_count, block_size, KVH, HD),
        value_piece.reshape(block_count, block_size, KVH, HD),
        key_pos.reshape(block_count, block_size),
    )
    final_state, unused = lax.scan(update, start_state, blocks)
    maxima, sums, accumulated = final_state
    has_key = maxima > -1e29
    safe_total = jnp.where(has_key, sums, 1.0)
    key_mask = jnp.transpose(has_key, (2, 0, 1))
    part = jnp.where(
        key_mask[..., None], accumulated / jnp.transpose(safe_total, (2, 0, 1))[..., None], 0.0
    )
    part = part.astype(jnp.bfloat16).reshape(query_count, KVH * GROUP * HD)
    log_total = jnp.where(key_mask, jnp.transpose(maxima + jnp.log(safe_total), (2, 0, 1)), -1e30)
    largest = lax.pmax(log_total.astype(jnp.bfloat16), "col").astype(log_total.dtype)
    raised = jnp.exp(log_total - largest)
    total = lax.psum(raised.astype(jnp.bfloat16), "col").astype(jnp.float32)
    weights = raised / total
    weighted = (
        part.reshape(query_count, KVH, GROUP, HD).astype(jnp.float32) * weights[..., None]
    ).reshape(query_count, KVH * GROUP * HD)
    merged = lax.psum_scatter(weighted.astype(jnp.bfloat16), "col", scatter_dimension=0, tiled=True)
    return merged


def solution(mesh):
    return jax.shard_map(
        shards,
        mesh=mesh,
        in_specs=(
            P("row", None),
            P(("row", "col"), None),
            P(("row", "col"), None),
            P(("row", "col")),
        ),
        out_specs=P(("row", "col"), None),
        check_vma=False,
    )
```

profile of v0, /device:TPU:1, one launch (start us, length us, event | category | flops | bytes accessed | tf_op | source)
XLA Modules:
  0.0 498.9 jit_solution(6404779670905542395)
XLA Ops:
  6.5 0.7 all-gather.3.cloned.1.call-update
  7.3 0.7 all-gather.5.cloned.1.call-update
  8.1 0.9 dynamic-update-slice
  9.0 113.9 %all-reduce = s32[8192]{0:T(1024)S(1)} all-reduce(s32[8192]{0:T(1024)S(1)} %dynamic-update-slice), channel_id=1, replica_groups=mesh['row'=64,'col'=8] {'row','col'}, use_global_device_ids=true, to_apply=%add | all-reduce | flops 8192 | bytes 65536
  123.8 0.7 reshape_reshape.3
  124.5 4.1 copy.9
  128.5 3.0 copy.12
  131.6 1.4 reshape.29
  133.0 85.1 %all-gather.5.cloned.1.call-done = bf16[1024,512]{1,0:T(8,128)(2,1)} async-done(((bf16[16,512]{1,0:T(8,128)(2,1)}), bf16[1024,512]{1,0:T(8,128)(2,1)}) %all-gather.5.cloned.1.call-update) | async-done | bytes 1048592 | tf_op jit(solution)/shard_map/all_gather | solution.py:53
  218.1 2.2 reshape.30
  220.4 109.8 %while.16 = (s32[]{:T(128)}, f32[4,16,128]{2,1,0:T(8,128)S(1)}, f32[4,16,128]{2,1,0:T(8,128)S(1)}, f32[128,4,16,128]{0,3,2,1:T(8,128)}, s32[8,128]{1,0:T(8,128)}...) while((s32[]{:T(128)}, f32[4,16,128]{2,1,0:T(8,128)S(1)}, ...), condition=%wide.wide.region_3.4_spmd.clone, body=%wide.wide.region_0.3_spmd.clone.sunk | while | flops 553713664 | bytes 41486500 | solution.py:62
  220.4 0.7 fusion.40
  221.1 0.8 broadcast_compare_fusion.4
  221.8 1.0 constant_dynamic-slice_fusion.5
  222.8 2.8 fusion.41
  225.8 5.9 %bitcast_add_fusion.3 = f32[128,4,16,128]{0,3,2,1:T(8,128)} fusion(f32[128,4,16,128]{0,3,2,1:T(8,128)} %get-tuple-element.250, f32[4,128,128,16]{2,1,3,0:T(8,128)} %get-tuple-element.232, f32[128,4,16]{0,2,1:T(8,128)S(1)} %get-tuple-element.233, f32[4,16,128]{2,1,0:T(8,128)S(1)} %get-tuple-element.260, pred[]{:T(512)S(6)} %compare.4, ...), kind=kOutput, calls=%fused_computation.clone.clone.1 | convolution fusion | flops 276824064 | bytes 12795905 | tf_op jit(solution)/shard_map/while/body/eval_jaxpr/grqk,kgd->qgrd/dot_general | solution.py:38
  231.6 1.3 fusion.43
  233.0 0.7 fusion.40
  233.7 0.8 broadcast_compare_fusion.4
  234.4 1.0 constant_dynamic-slice_fusion.5
  235.4 2.8 fusion.41
  238.4 7.1 %bitcast_add_fusion.3 = f32[128,4,16,128]{0,3,2,1:T(8,128)} fusion(f32[128,4,16,128]{0,3,2,1:T(8,128)} %get-tuple-element.250, f32[4,128,128,16]{2,1,3,0:T(8,128)} %get-tuple-element.232, f32[128,4,16]{0,2,1:T(8,128)S(1)} %get-tuple-element.233, f32[4,16,128]{2,1,0:T(8,128)S(1)} %get-tuple-element.260, pred[]{:T(512)S(6)} %compare.4, ...), kind=kOutput, calls=%fused_computation.clone.clone.1 | convolution fusion | flops 276824064 | bytes 12795905 | tf_op jit(solution)/shard_map/while/body/eval_jaxpr/grqk,kgd->qgrd/dot_general | solution.py:38
  245.5 1.3 fusion.43
  246.9 0.7 fusion.40
  247.6 0.8 broadcast_compare_fusion.4
  248.3 1.0 constant_dynamic-slice_fusion.5
  249.3 2.8 fusion.41
  252.3 7.1 %bitcast_add_fusion.3 = f32[128,4,16,128]{0,3,2,1:T(8,128)} fusion(f32[128,4,16,128]{0,3,2,1:T(8,128)} %get-tuple-element.250, f32[4,128,128,16]{2,1,3,0:T(8,128)} %get-tuple-element.232, f32[128,4,16]{0,2,1:T(8,128)S(1)} %get-tuple-element.233, f32[4,16,128]{2,1,0:T(8,128)S(1)} %get-tuple-element.260, pred[]{:T(512)S(6)} %compare.4, ...), kind=kOutput, calls=%fused_computation.clone.clone.1 | convolution fusion | flops 276824064 | bytes 12795905 | tf_op jit(solution)/shard_map/while/body/eval_jaxpr/grqk,kgd->qgrd/dot_general | solution.py:38
  259.4 1.3 fusion.43
  260.8 0.7 fusion.40
  261.4 0.8 broadcast_compare_fusion.4
  262.2 1.0 constant_dynamic-slice_fusion.5
  263.2 2.8 fusion.41
  266.2 7.1 %bitcast_add_fusion.3 = f32[128,4,16,128]{0,3,2,1:T(8,128)} fusion(f32[128,4,16,128]{0,3,2,1:T(8,128)} %get-tuple-element.250, f32[4,128,128,16]{2,1,3,0:T(8,128)} %get-tuple-element.232, f32[128,4,16]{0,2,1:T(8,128)S(1)} %get-tuple-element.233, f32[4,16,128]{2,1,0:T(8,128)S(1)} %get-tuple-element.260, pred[]{:T(512)S(6)} %compare.4, ...), kind=kOutput, calls=%fused_computation.clone.clone.1 | convolution fusion | flops 276824064 | bytes 12795905 | tf_op jit(solution)/shard_map/while/body/eval_jaxpr/grqk,kgd->qgrd/dot_general | solution.py:38
  273.3 1.3 fusion.43
  274.6 0.7 fusion.40
  275.3 0.8 broadcast_compare_fusion.4
  276.1 1.0 constant_dynamic-slice_fusion.5
  277.1 2.8 fusion.41
  280.0 7.1 %bitcast_add_fusion.3 = f32[128,4,16,128]{0,3,2,1:T(8,128)} fusion(f32[128,4,16,128]{0,3,2,1:T(8,128)} %get-tuple-element.250, f32[4,128,128,16]{2,1,3,0:T(8,128)} %get-tuple-element.232, f32[128,4,16]{0,2,1:T(8,128)S(1)} %get-tuple-element.233, f32[4,16,128]{2,1,0:T(8,128)S(1)} %get-tuple-element.260, pred[]{:T(512)S(6)} %compare.4, ...), kind=kOutput, calls=%fused_computation.clone.clone.1 | convolution fusion | flops 276824064 | bytes 12795905 | tf_op jit(solution)/shard_map/while/body/eval_jaxpr/grqk,kgd->qgrd/dot_general | solution.py:38
  287.2 1.3 fusion.43
  288.5 0.7 fusion.40
  289.2 0.8 broadcast_compare_fusion.4
  290.0 1.0 constant_dynamic-slice_fusion.5
  291.0 2.8 fusion.41
  293.9 7.1 %bitcast_add_fusion.3 = f32[128,4,16,128]{0,3,2,1:T(8,128)} fusion(f32[128,4,16,128]{0,3,2,1:T(8,128)} %get-tuple-element.250, f32[4,128,128,16]{2,1,3,0:T(8,128)} %get-tuple-element.232, f32[128,4,16]{0,2,1:T(8,128)S(1)} %get-tuple-element.233, f32[4,16,128]{2,1,0:T(8,128)S(1)} %get-tuple-element.260, pred[]{:T(512)S(6)} %compare.4, ...), kind=kOutput, calls=%fused_computation.clone.clone.1 | convolution fusion | flops 276824064 | bytes 12795905 | tf_op jit(solution)/shard_map/while/body/eval_jaxpr/grqk,kgd->qgrd/dot_general | solution.py:38
  301.1 1.3 fusion.43
  302.4 0.7 fusion.40
  303.1 0.8 broadcast_compare_fusion.4
  303.9 1.0 constant_dynamic-slice_fusion.5
  304.9 2.8 fusion.41
  307.8 7.1 %bitcast_add_fusion.3 = f32[128,4,16,128]{0,3,2,1:T(8,128)} fusion(f32[128,4,16,128]{0,3,2,1:T(8,128)} %get-tuple-element.250, f32[4,128,128,16]{2,1,3,0:T(8,128)} %get-tuple-element.232, f32[128,4,16]{0,2,1:T(8,128)S(1)} %get-tuple-element.233, f32[4,16,128]{2,1,0:T(8,128)S(1)} %get-tuple-element.260, pred[]{:T(512)S(6)} %compare.4, ...), kind=kOutput, calls=%fused_computation.clone.clone.1 | convolution fusion | flops 276824064 | bytes 12795905 | tf_op jit(solution)/shard_map/while/body/eval_jaxpr/grqk,kgd->qgrd/dot_general | solution.py:38
  314.9 1.3 fusion.43
  316.3 0.7 fusion.40
  317.0 0.8 broadcast_compare_fusion.4
  317.8 1.0 constant_dynamic-slice_fusion.5
  318.8 2.8 fusion.41
  321.7 7.1 %bitcast_add_fusion.3 = f32[128,4,16,128]{0,3,2,1:T(8,128)} fusion(f32[128,4,16,128]{0,3,2,1:T(8,128)} %get-tuple-element.250, f32[4,128,128,16]{2,1,3,0:T(8,128)} %get-tuple-element.232, f32[128,4,16]{0,2,1:T(8,128)S(1)} %get-tuple-element.233, f32[4,16,128]{2,1,0:T(8,128)S(1)} %get-tuple-element.260, pred[]{:T(512)S(6)} %compare.4, ...), kind=kOutput, calls=%fused_computation.clone.clone.1 | convolution fusion | flops 276824064 | bytes 12795905 | tf_op jit(solution)/shard_map/while/body/eval_jaxpr/grqk,kgd->qgrd/dot_general | solution.py:38
  328.8 1.3 fusion.43
  330.2 42.6 %pmax.7 = bf16[128,4,16]{0,2,1:T(8,128)(2,1)S(1)} all-reduce(bf16[128,4,16]{0,2,1:T(8,128)(2,1)S(1)} %fusion.19), channel_id=1, replica_groups=mesh['row'=64,'col'=8] {'col'}, use_global_device_ids=true, to_apply=%region_4.5 | all-reduce | flops 8192 | bytes 32768 | tf_op jit(solution)/shard_map/pmax | solution.py:72
  372.8 42.0 %psum.7 = bf16[128,4,16]{0,2,1:T(8,128)(2,1)S(1)} all-reduce(bf16[128,4,16]{0,2,1:T(8,128)(2,1)S(1)} %fusion.17), channel_id=1, replica_groups=mesh['row'=64,'col'=8] {'col'}, use_global_device_ids=true, to_apply=%region_5.6 | all-reduce | flops 8192 | bytes 32768 | tf_op jit(solution)/shard_map/psum | solution.py:74
  414.9 3.3 multiply_convert_fusion
  418.2 3.0 copy.22
  421.2 71.1 %reduce-scatter.2.cloned.1.call-done = bf16[16,8192]{1,0:T(8,128)(2,1)} async-done(((bf16[128,8192]{1,0:T(8,128)(2,1)}), bf16[16,8192]{1,0:T(8,128)(2,1)}) %reduce-scatter.2.cloned.1.call-update) | async-done | bytes 262160 | tf_op jit(solution)/shard_map/reduce_scatter | solution.py:79
  (68 shorter events, 2.6 us)
Async XLA Ops:
  6.5 125.1 %all-gather.3.cloned.1.call-start = ((), (), s32[]{:S(2)}) async-start(), calls=%async_computation.1 | async-start | bytes 1064960 | tf_op jit(solution)/shard_map/all_gather | solution.py:52
  7.3 210.9 %all-gather.5.cloned.1.call-start = ((), (), s32[]{:S(2)}) async-start(), calls=%async_computation.2 | async-start | bytes 1064960 | tf_op jit(solution)/shard_map/all_gather | solution.py:53
  8.0 484.3 %reduce-scatter.2.cloned.1.call-start = ((), (), s32[]{:S(2)}) async-start(), calls=%async_computation.3 | async-start | bytes 2359296 | tf_op jit(solution)/shard_map/reduce_scatter | solution.py:79
  123.0 0.7 copy-start.1
  225.8 5.9 %copy-start = (f32[4,128,128,16]{2,1,3,0:T(8,128)S(1)}, f32[4,128,128,16]{2,1,3,0:T(8,128)}, u32[]{:S(2)}) copy-start(f32[4,128,128,16]{2,1,3,0:T(8,128)} %get-tuple-element.232) | copy-start | bytes 12582916 | tf_op jit(solution)/shard_map/while
  238.4 7.1 %copy-start = (f32[4,128,128,16]{2,1,3,0:T(8,128)S(1)}, f32[4,128,128,16]{2,1,3,0:T(8,128)}, u32[]{:S(2)}) copy-start(f32[4,128,128,16]{2,1,3,0:T(8,128)} %get-tuple-element.232) | copy-start | bytes 12582916 | tf_op jit(solution)/shard_map/while
  252.3 7.1 %copy-start = (f32[4,128,128,16]{2,1,3,0:T(8,128)S(1)}, f32[4,128,128,16]{2,1,3,0:T(8,128)}, u32[]{:S(2)}) copy-start(f32[4,128,128,16]{2,1,3,0:T(8,128)} %get-tuple-element.232) | copy-start | bytes 12582916 | tf_op jit(solution)/shard_map/while
  266.2 7.1 %copy-start = (f32[4,128,128,16]{2,1,3,0:T(8,128)S(1)}, f32[4,128,128,16]{2,1,3,0:T(8,128)}, u32[]{:S(2)}) copy-start(f32[4,128,128,16]{2,1,3,0:T(8,128)} %get-tuple-element.232) | copy-start | bytes 12582916 | tf_op jit(solution)/shard_map/while
  280.0 7.1 %copy-start = (f32[4,128,128,16]{2,1,3,0:T(8,128)S(1)}, f32[4,128,128,16]{2,1,3,0:T(8,128)}, u32[]{:S(2)}) copy-start(f32[4,128,128,16]{2,1,3,0:T(8,128)} %get-tuple-element.232) | copy-start | bytes 12582916 | tf_op jit(solution)/shard_map/while
  293.9 7.1 %copy-start = (f32[4,128,128,16]{2,1,3,0:T(8,128)S(1)}, f32[4,128,128,16]{2,1,3,0:T(8,128)}, u32[]{:S(2)}) copy-start(f32[4,128,128,16]{2,1,3,0:T(8,128)} %get-tuple-element.232) | copy-start | bytes 12582916 | tf_op jit(solution)/shard_map/while
  307.8 7.1 %copy-start = (f32[4,128,128,16]{2,1,3,0:T(8,128)S(1)}, f32[4,128,128,16]{2,1,3,0:T(8,128)}, u32[]{:S(2)}) copy-start(f32[4,128,128,16]{2,1,3,0:T(8,128)} %get-tuple-element.232) | copy-start | bytes 12582916 | tf_op jit(solution)/shard_map/while
  321.7 7.1 %copy-start = (f32[4,128,128,16]{2,1,3,0:T(8,128)S(1)}, f32[4,128,128,16]{2,1,3,0:T(8,128)}, u32[]{:S(2)}) copy-start(f32[4,128,128,16]{2,1,3,0:T(8,128)} %get-tuple-element.232) | copy-start | bytes 12582916 | tf_op jit(solution)/shard_map/while
Sparse Core Ops, SparseCore 0:
  11.8 109.4 all-gather.2
  125.7 92.3 all-gather.4
  421.3 70.9 reduce-scatter.1
where the time goes:
time: 504 us; the launch traced here: 499 us
  blocking collectives  198 us (39%)
  waiting for transfers between devices  158 us (31%)
  matrix products  77.9 us (15%)
  local copies, waits for them, and re-layouts  30.9 us (6%)
  other arithmetic  20.1 us (4%)
  between operations  13.3 us (3%)
    unnamed x1, blocking collectives  114 us
    all_gather x1, waiting for transfers between devices, shards(): value_piece = lax.all_gather(values, 'row', axis=0, tiled=True)  85.1 us
    reduce_scatter x1, waiting for transfers between devices, shards(): lax.psum_scatter(weighted.astype(jnp.bfloat16), 'col', scatter_dimension=...  71.1 us
    dot_general x8, matrix products, update(): jnp.einsum('grqk,kgd->qgrd', raised.astype(jnp.bfloat16), value_block, pr...  55.7 us
    pmax x1, blocking collectives, shards(): lax.pmax(log_total.astype(jnp.bfloat16), 'col').astype(log_total.dtype)  42.6 us
    psum x1, blocking collectives, shards(): total = lax.psum(raised.astype(jnp.bfloat16), 'col').astype(jnp.float32)  42 us
    dot_general x8, matrix products, update(): jnp.einsum('qgrd,kgd->grqk', grouped, key_block, preferred_element_type=j...  22.2 us
    reduce_sum x8, other arithmetic, update(): new_sum = running_sum * rescale + raised.sum(-1)  10.3 us
  transfers between devices with their start and end apart: 3, of which 2 were waited for; matrix products, arithmetic and copies ran while one was open for 2% of the time, Pallas kernels for 0%

commit v1 on v0

v1 whole, which is shorter than its diff:
```python
import math

import jax
import jax.numpy as jnp
from jax import lax
from jax.experimental import pallas as pl
from jax.experimental.pallas import tpu as pltpu
from jax.sharding import PartitionSpec as P

HD = 128
KVH = 4
GROUP = 16
TOK = 16
NX, NY, NZ, NLO = 4, 4, 16, 8
QTOK = 64
WIDTH = GROUP * HD
BLOCK = 2 * NZ + 1
KEYS = 2 * NZ * TOK
BF = jnp.bfloat16
F32 = jnp.float32
MASKED = -1e30
RATE = math.log2(math.e) / math.sqrt(HD)

ORDER = [
    (0, 0), (1, 0), (3, 0), (0, 1), (0, 3), (2, 0), (1, 1), (1, 3),
    (3, 1), (3, 3), (0, 2), (2, 1), (2, 3), (1, 2), (3, 2), (2, 2),
]
SLOT = {place: index for index, place in enumerate(ORDER)}
STEP = {"A-": (1, 0), "A+": (-1, 0), "B-": (0, 1), "B+": (0, -1)}
FORWARD = {
    (0, 0): ["A-", "A+", "B-", "B+"],
    (1, 0): ["A-", "B-", "B+"],
    (3, 0): ["B-", "B+"],
    (2, 0): ["B-", "B+"],
    (0, 1): ["B-"],
    (1, 1): ["B-"],
    (2, 3): ["B+"],
    (3, 3): ["B+"],
}
ROUTES = []
for place in ORDER:
    for way in FORWARD.get(place, []):
        da, db = STEP[way]
        ROUTES.append((SLOT[place], way, SLOT[((place[0] + da) % 4, (place[1] + db) % 4)]))


def kernel(
    q_hbm, k_ref, v_ref, order_ref, out_ref,
    mine, theirs, stage, pos_own, pos_line, q_raw, q_t, k_aug, v_rows, v_t, acc, top, out_stage,
    q_sem, z_send, z_recv, p_send, p_recv, f_send, m_recv, c_send, t_recv, o_send, o_recv,
):
    row = lax.axis_index("row")
    col = lax.axis_index("col")
    core = row % 2
    x = (row // 2) % NX
    y = row // (4 * NX)
    z = ((row // (2 * NX)) % 2) * NLO + col
    head = col % KVH
    half = col // KVH

    def device(x_at, y_at, z_at, core_at):
        return (y_at * (4 * NX) + (z_at // NLO) * (2 * NX) + x_at * 2 + core_at, z_at % NLO)

    line = [None] + [device(x, y, (z + d) % NZ, core) for d in range(1, NZ)]
    plane = {}
    for way, (da, db) in STEP.items():
        sx = (1 - core) * da + core * db
        sy = core * da + (1 - core) * db
        plane[way] = device((x - sx + NX) % NX, (y - sy + NY) % NY, z, core)
    twin = device(x, y, z, 1 - core)

    q_copy = pltpu.make_async_copy(
        q_hbm.at[pl.ds(half * QTOK, QTOK), pl.ds(pl.multiple_of(head * WIDTH, WIDTH), WIDTH)],
        q_raw, q_sem,
    )
    q_copy.start()

    barrier = pltpu.get_barrier_semaphore()
    others = line[1:] + list(plane.values()) + [twin]
    for other in others:
        pl.semaphore_signal(barrier, inc=1, device_id=other, device_id_type=pl.DeviceIdType.MESH)

    for g in range(KVH):
        stage[g, 0] = k_ref[:, g * HD:(g + 1) * HD]
        stage[g, 1] = v_ref[:, g * HD:(g + 1) * HD]
    pos_own[...] = jnp.full((1, 128), order_ref[0], jnp.int32)

    pl.semaphore_wait(barrier, len(others))

    def remote(src, dst, send, recv, to):
        return pltpu.make_async_remote_copy(
            src_ref=src, dst_ref=dst, send_sem=send, recv_sem=recv,
            device_id=to, device_id_type=pl.DeviceIdType.MESH,
        )

    line_copies = []
    for n, d in enumerate([8, 7, 9, 6, 10, 5, 11, 4, 12, 3, 13, 2, 14, 1, 15]):
        at = NZ - d
        line_copies.append(remote(
            stage.at[(z + d) % KVH], mine.at[0, pl.ds(2 * at, 2)], z_send.at[n], z_recv, line[d]
        ))
        line_copies.append(remote(
            pos_own, pos_line.at[at], p_send.at[n], p_recv, line[d]
        ))
    for copy in line_copies:
        copy.start()
    mine[0, 0:2] = stage[head]
    pos_line[0] = pos_own[...]

    q_copy.wait()
    for cc in range(4):
        rows = jnp.concatenate(
            [q_raw[cc * TOK:(cc + 1) * TOK, g * HD:(g + 1) * HD] for g in range(GROUP)], axis=0
        )
        q_t[0:HD, cc * 256:(cc + 1) * 256] = rows.T
        token = lax.broadcasted_iota(jnp.int32, (HD, 256), 0)
        lane = lax.broadcasted_iota(jnp.int32, (HD, 256), 1)
        q_t[HD:, cc * 256:(cc + 1) * 256] = jnp.where(
            token == cc * TOK + lane % TOK, 1.0, 0.0
        ).astype(BF)
    v_t[HD:, :] = jnp.ones((TOK, KEYS), BF)
    acc[...] = jnp.zeros_like(acc)
    top[...] = jnp.full_like(top, MASKED)

    pltpu.make_async_copy(pos_line.at[pl.ds(1, NZ - 1)], pos_line.at[pl.ds(1, NZ - 1)], p_recv).wait()
    starts = jnp.concatenate([pos_line[d] for d in range(NZ)], axis=0)
    lane16 = lax.broadcasted_iota(jnp.int32, (TOK, 128), 1)
    mine[0, 2 * NZ] = jnp.where(lane16 < 64, starts // 128, starts % 128).astype(F32).astype(BF)
    lane1 = lax.broadcasted_iota(jnp.int32, (1, 128), 1)
    q_pos = jnp.zeros((1, 128), jnp.int32)
    for cc in range(4):
        q_pos = jnp.where(
            lane1 // TOK == cc, pos_line[(cc - head + NZ) % NZ] + lane1 % TOK, q_pos
        )
    q_pos = q_pos.astype(F32)

    pltpu.make_async_copy(
        mine.at[0, pl.ds(2, 2 * NZ - 2)], mine.at[0, pl.ds(2, 2 * NZ - 2)], z_recv
    ).wait()

    def route(n):
        slot, way, there = ROUTES[n]
        return remote(mine.at[slot], mine.at[there], f_send.at[n], m_recv.at[there], plane[way])

    def to_twin(slot):
        return remote(mine.at[slot], theirs.at[slot], c_send.at[slot], t_recv.at[slot], twin)

    for n in range(len(ROUTES)):
        if ROUTES[n][0] == 0:
            route(n).start()
    to_twin(0).start()

    def prepare(block, slot, base):
        word = block[slot, 2 * NZ].astype(F32)
        turned = pltpu.roll(word, 64, 1)
        start = jnp.where(lane16 < 64, word * 128.0 + turned, turned * 128.0 + word)
        offset = lax.broadcasted_iota(jnp.int32, (TOK, 128), 0).astype(F32)
        for d in range(NZ):
            at = slice(base + d * TOK, base + (d + 1) * TOK)
            k_aug[at, 0:HD] = block[slot, 2 * d]
            k_pos = start[d:d + 1, :] + offset
            k_aug[at, HD:] = jnp.where(k_pos <= q_pos, 0.0, MASKED).astype(BF)
            v_rows[at, :] = block[slot, 2 * d + 1]
        part = slice(base, base + NZ * TOK)
        v_t[0:HD, part] = v_rows[part, :].T

    def step(slot, carry):
        @pl.when(slot < 15)
        def _():
            later = mine.at[slot + 1]
            pltpu.make_async_copy(later, later, m_recv.at[slot + 1]).wait()
            for n in range(len(ROUTES)):
                if ROUTES[n][0] > 0:
                    @pl.when(slot + 1 == ROUTES[n][0])
                    def _():
                        route(n).start()
            to_twin(slot + 1).start()

        prepare(mine, slot, 0)
        pltpu.make_async_copy(theirs.at[slot], theirs.at[slot], t_recv.at[slot]).wait()
        prepare(theirs, slot, NZ * TOK)
        for cc in range(4):
            at = slice(cc * 256, (cc + 1) * 256)
            scores = jnp.dot(k_aug[...], q_t[:, at], preferred_element_type=F32)
            old = top[:, at]
            new = jnp.maximum(old, jnp.max(scores, axis=0, keepdims=True))
            probs = jnp.exp2((scores - new) * RATE).astype(BF)
            acc[:, at] = acc[:, at] * jnp.exp2((old - new) * RATE) + jnp.dot(
                v_t[...], probs, preferred_element_type=F32
            )
            top[:, at] = new
        return carry

    lax.fori_loop(0, 16, step, 0)

    for cc in range(4):
        at = slice(cc * 256, (cc + 1) * 256)
        done = (acc[0:HD, at] / acc[HD:HD + 1, at]).T.astype(BF)
        for g in range(GROUP):
            out_stage[cc, :, g * HD:(g + 1) * HD] = done[g * TOK:(g + 1) * TOK, :]
    columns = pl.ds(pl.multiple_of(head * WIDTH, WIDTH), WIDTH)
    out_copies = []
    for j in (2, 1, 3):
        cc = (head + j) % KVH
        to = device(x, y, (z // KVH) * KVH + cc, core)
        out_copies.append(remote(
            out_stage.at[cc], out_ref.at[:, columns], o_send.at[j], o_recv.at[j], to
        ))
    for copy in out_copies:
        copy.start()
    own = pltpu.make_async_copy(out_stage.at[head], out_ref.at[:, columns], o_send.at[0])
    own.start()
    own.wait()
    for j in (1, 2, 3):
        source = (head - j + KVH) % KVH
        place = out_ref.at[:, pl.ds(pl.multiple_of(source * WIDTH, WIDTH), WIDTH)]
        pltpu.make_async_copy(place, place, o_recv.at[j]).wait()
    for copy in out_copies:
        copy.wait_send()
    for copy in line_copies:
        copy.wait_send()
    for n in range(len(ROUTES)):
        route(n).wait_send()
    for slot in range(16):
        to_twin(slot).wait_send()


def shards(queries, keys, values, order):
    dma = pltpu.SemaphoreType.DMA
    return pl.pallas_call(
        kernel,
        out_shape=jax.ShapeDtypeStruct((TOK, KVH * WIDTH), BF),
        in_specs=[
            pl.BlockSpec(memory_space=pl.ANY),
            pl.BlockSpec(memory_space=pltpu.VMEM),
            pl.BlockSpec(memory_space=pltpu.VMEM),
            pl.BlockSpec(memory_space=pltpu.SMEM),
        ],
        out_specs=pl.BlockSpec(memory_space=pltpu.VMEM),
        scratch_shapes=[
            pltpu.VMEM((16, BLOCK, TOK, HD), BF),
            pltpu.VMEM((16, BLOCK, TOK, HD), BF),
            pltpu.VMEM((KVH, 2, TOK, HD), BF),
            pltpu.VMEM((1, 128), jnp.int32),
            pltpu.VMEM((NZ, 1, 128), jnp.int32),
            pltpu.VMEM((QTOK, WIDTH), BF),
            pltpu.VMEM((2 * HD, 1024), BF),
            pltpu.VMEM((KEYS, 2 * HD), BF),
            pltpu.VMEM((KEYS, HD), BF),
            pltpu.VMEM((HD + TOK, KEYS), BF),
            pltpu.VMEM((HD + TOK, 1024), F32),
            pltpu.VMEM((1, 1024), F32),
            pltpu.VMEM((4, TOK, WIDTH), BF),
            dma, dma((NZ - 1,)), dma, dma((NZ - 1,)), dma,
            dma((len(ROUTES),)), dma((16,)), dma((16,)), dma((16,)), dma((4,)), dma((4,)),
        ],
        compiler_params=pltpu.CompilerParams(
            collective_id=0, has_side_effects=True, vmem_limit_bytes=40 * 1024 * 1024
        ),
        cost_estimate=pl.CostEstimate(
            flops=4 * 1024 * 8192 * 128, bytes_accessed=1 << 20, transcendentals=1024 * 8192
        ),
    )(queries, keys, values, order)


def solution(mesh):
    return jax.shard_map(
        shards,
        mesh=mesh,
        in_specs=(
            P("row", None),
            P(("row", "col"), None),
            P(("row", "col"), None),
            P(("row", "col")),
        ),
        out_specs=P(("row", "col"), None),
        check_vma=False,
    )
```

time: 504 us -> 71.7 us (0.14)
  the two profiles are of different devices: /device:TPU:1 before, /device:TPU:2 now
where the time goes in v1:
time: 71.7 us; the launch traced here: 71.4 us
  Pallas kernels  67 us (93%)
  local copies, waits for them, and re-layouts  4.38 us (6%)
    pallas_call x1, Pallas kernels, shards(): pl.pallas_call(kernel, out_shape=jax.ShapeDtypeStruct((TOK, KVH * WIDTH),...  67 us
    unnamed x9, local copies, waits for them, and re-layouts  4.38 us

profile of v1, /device:TPU:2, one launch (start us, length us, event | category | flops | bytes accessed | tf_op | source)
XLA Modules:
  0.0 71.4 jit_solution(16857216345162249996)
XLA Ops:
  0.0 0.0 copy-start
  0.0 1.6 %copy-done = bf16[128,8192]{1,0:T(8,128)(2,1)S(1)} copy-done((bf16[128,8192]{1,0:T(8,128)(2,1)S(1)}, bf16[128,8192]{1,0:T(8,128)(2,1)}, u32[]{:S(2)}) %copy-start) | copy-done | bytes 2097176
  1.6 0.0 copy-start.1
  1.6 0.7 %copy-done.1 = bf16[16,512]{1,0:T(8,128)(2,1)S(1)} copy-done((bf16[16,512]{1,0:T(8,128)(2,1)S(1)}, bf16[16,512]{1,0:T(8,128)(2,1)}, u32[]{:S(2)}) %copy-start.1) | copy-done | bytes 16408
  2.3 0.0 copy-start.2
  2.3 0.7 %copy-done.2 = bf16[16,512]{1,0:T(8,128)(2,1)S(1)} copy-done((bf16[16,512]{1,0:T(8,128)(2,1)S(1)}, bf16[16,512]{1,0:T(8,128)(2,1)}, u32[]{:S(2)}) %copy-start.2) | copy-done | bytes 16408
  3.0 0.0 copy-start.3
  3.0 0.7 copy-done.3
  3.7 67.0 %shard_map.46 = bf16[16,8192]{1,0:T(8,128)(2,1)S(1)} custom-call(bf16[128,8192]{1,0:T(8,128)(2,1)S(1)} %copy-done, bf16[16,512]{1,0:T(8,128)(2,1)S(1)} %copy-done.1, bf16[16,512]{1,0:T(8,128)(2,1)S(1)} %copy-done.2, s32[16]{0:T(128)S(1)} %copy-done.3), custom_call_target="tpu_custom_call" | custom-call | flops 4294967296 | bytes 1048576 | tf_op jit(solution)/shard_map/pallas_call | solution.py:230
  70.7 0.7 copy.6
Async XLA Ops:
  0.0 1.6 %copy-start = (bf16[128,8192]{1,0:T(8,128)(2,1)S(1)}, bf16[128,8192]{1,0:T(8,128)(2,1)}, u32[]{:S(2)}) copy-start(bf16[128,8192]{1,0:T(8,128)(2,1)} %q_hbm.1) | copy-start | bytes 6291460
  1.6 0.7 %copy-start.1 = (bf16[16,512]{1,0:T(8,128)(2,1)S(1)}, bf16[16,512]{1,0:T(8,128)(2,1)}, u32[]{:S(2)}) copy-start(bf16[16,512]{1,0:T(8,128)(2,1)} %k_ref.1) | copy-start | bytes 49156
  2.3 0.7 %copy-start.2 = (bf16[16,512]{1,0:T(8,128)(2,1)S(1)}, bf16[16,512]{1,0:T(8,128)(2,1)}, u32[]{:S(2)}) copy-start(bf16[16,512]{1,0:T(8,128)(2,1)} %v_ref.1) | copy-start | bytes 49156
  3.0 0.7 copy-start.3

commit v2 on v1

v2 whole, which is shorter than its diff:
```python
import math

import jax
import jax.numpy as jnp
from jax import lax
from jax.experimental import pallas as pl
from jax.experimental.pallas import tpu as pltpu
from jax.sharding import PartitionSpec as P

HD = 128
KVH = 4
GROUP = 16
TOK = 16
NX, NY, NZ, NLO = 4, 4, 16, 8
QTOK = 64
WIDTH = GROUP * HD
BLOCK = 2 * 2 * HD + TOK
KEYS = 2 * NZ * TOK
BF = jnp.bfloat16
F32 = jnp.float32
MASKED = -1e30
RATE = math.log2(math.e) / math.sqrt(HD)

ORDER = [
    (0, 0), (1, 0), (3, 0), (0, 1), (0, 3), (2, 0), (1, 1), (1, 3),
    (3, 1), (3, 3), (0, 2), (2, 1), (2, 3), (1, 2), (3, 2), (2, 2),
]
SLOT = {place: index for index, place in enumerate(ORDER)}
STEP = {"A-": (1, 0), "A+": (-1, 0), "B-": (0, 1), "B+": (0, -1)}
FORWARD = {
    (0, 0): ["A-", "A+", "B-", "B+"],
    (1, 0): ["A-", "B-", "B+"],
    (3, 0): ["B-", "B+"],
    (2, 0): ["B-", "B+"],
    (0, 1): ["B-"],
    (1, 1): ["B-"],
    (2, 3): ["B+"],
    (3, 3): ["B+"],
}
ROUTES = []
for place in ORDER:
    for way in FORWARD.get(place, []):
        da, db = STEP[way]
        ROUTES.append((SLOT[place], way, SLOT[((place[0] + da) % 4, (place[1] + db) % 4)]))


def kernel(
    q_hbm, k_hbm, v_hbm, order_hbm, out_ref,
    mine, theirs, stage, landed, order_own, pos_own, pos_line, q_raw, q_t,
    even, odd, peak_even, peak_odd, acc, top, out_stage,
    q_sem, kv_sem, order_sem,
    z_send, z_recv, p_send, p_recv, f_send, m_recv, c_send, t_recv, o_send, o_recv,
):
    row = lax.axis_index("row")
    col = lax.axis_index("col")
    core = row % 2
    x = (row // 2) % NX
    y = row // (4 * NX)
    z = ((row // (2 * NX)) % 2) * NLO + col
    head = col % KVH
    half = col // KVH

    order_copy = pltpu.make_async_copy(order_hbm, order_own, order_sem)
    order_copy.start()
    for g in range(KVH):
        columns = slice(g * HD, (g + 1) * HD)
        pltpu.make_async_copy(k_hbm.at[:, columns], stage.at[g, 0], kv_sem).start()
        pltpu.make_async_copy(v_hbm.at[:, columns], stage.at[g, 1], kv_sem).start()
    q_copy = pltpu.make_async_copy(
        q_hbm.at[pl.ds(half * QTOK, QTOK), pl.ds(pl.multiple_of(head * WIDTH, WIDTH), WIDTH)],
        q_raw, q_sem,
    )
    q_copy.start()

    def device(x_at, y_at, z_at, core_at):
        return (y_at * (4 * NX) + (z_at // NLO) * (2 * NX) + x_at * 2 + core_at, z_at % NLO)

    line = [None] + [device(x, y, (z + d) % NZ, core) for d in range(1, NZ)]
    plane = {}
    for way, (da, db) in STEP.items():
        sx = (1 - core) * da + core * db
        sy = core * da + (1 - core) * db
        plane[way] = device((x - sx + NX) % NX, (y - sy + NY) % NY, z, core)
    twin = device(x, y, z, 1 - core)

    barrier = pltpu.get_barrier_semaphore()
    others = line[1:] + list(plane.values()) + [twin]
    for other in others:
        pl.semaphore_signal(barrier, inc=1, device_id=other, device_id_type=pl.DeviceIdType.MESH)

    order_copy.wait()
    pos_own[...] = jnp.full((1, 128), order_own[0], jnp.int32)
    pltpu.make_async_copy(stage, stage, kv_sem).wait()
    pl.semaphore_wait(barrier, len(others))

    def remote(src, dst, send, recv, to):
        return pltpu.make_async_remote_copy(
            src_ref=src, dst_ref=dst, send_sem=send, recv_sem=recv,
            device_id=to, device_id_type=pl.DeviceIdType.MESH,
        )

    line_copies = []
    for n, d in enumerate([8, 7, 9, 6, 10, 5, 11, 4, 12, 3, 13, 2, 14, 1, 15]):
        at = NZ - d
        line_copies.append(remote(
            stage.at[(z + d) % KVH], landed.at[at], z_send.at[n], z_recv, line[d]
        ))
        line_copies.append(remote(
            pos_own, pos_line.at[at], p_send.at[n], p_recv, line[d]
        ))
    for copy in line_copies:
        copy.start()
    landed[0] = stage[head]
    pos_line[0] = pos_own[...]

    q_copy.wait()
    for cc in range(4):
        rows = jnp.concatenate(
            [q_raw[cc * TOK:(cc + 1) * TOK, g * HD:(g + 1) * HD] for g in range(GROUP)], axis=0
        )
        q_t[0:HD, cc * 256:(cc + 1) * 256] = rows.T
        token = lax.broadcasted_iota(jnp.int32, (HD, 256), 0)
        lane = lax.broadcasted_iota(jnp.int32, (HD, 256), 1)
        q_t[HD:, cc * 256:(cc + 1) * 256] = jnp.where(
            token == cc * TOK + lane % TOK, 1.0, 0.0
        ).astype(BF)
    acc[...] = jnp.zeros_like(acc)
    top[...] = jnp.full_like(top, MASKED)

    pltpu.make_async_copy(pos_line.at[pl.ds(1, NZ - 1)], pos_line.at[pl.ds(1, NZ - 1)], p_recv).wait()
    starts = jnp.concatenate([pos_line[d] for d in range(NZ)], axis=0)
    lane16 = lax.broadcasted_iota(jnp.int32, (TOK, 128), 1)
    mine[0, 4 * HD:] = jnp.where(lane16 < 64, starts // 128, starts % 128).astype(F32).astype(BF)
    lane1 = lax.broadcasted_iota(jnp.int32, (1, 128), 1)
    q_pos = jnp.zeros((1, 128), jnp.int32)
    for cc in range(4):
        q_pos = jnp.where(
            lane1 // TOK == cc, pos_line[(cc - head + NZ) % NZ] + lane1 % TOK, q_pos
        )
    q_pos = q_pos.astype(F32)

    rest = landed.at[pl.ds(1, NZ - 1)]
    pltpu.make_async_copy(rest, rest, z_recv).wait()
    for d in range(NZ):
        mine[0, d * TOK:(d + 1) * TOK] = landed[d, 0]
    for part in range(2):
        values = jnp.concatenate([landed[part * 8 + d, 1] for d in range(8)], axis=0)
        mine[0, (2 + part) * HD:(3 + part) * HD] = values.T

    def route(n):
        slot, way, there = ROUTES[n]
        return remote(mine.at[slot], mine.at[there], f_send.at[n], m_recv.at[there], plane[way])

    def to_twin(slot):
        return remote(mine.at[slot], theirs.at[slot], c_send.at[slot], t_recv.at[slot], twin)

    def wait_mine(slot):
        pltpu.make_async_copy(mine.at[slot], mine.at[slot], m_recv.at[slot]).wait()

    def wait_theirs(slot):
        pltpu.make_async_copy(theirs.at[slot], theirs.at[slot], t_recv.at[slot]).wait()

    def pass_on(slot):
        for n in range(len(ROUTES)):
            if isinstance(slot, int):
                if ROUTES[n][0] == slot:
                    route(n).start()
            elif ROUTES[n][0] > 1:
                @pl.when(slot == ROUTES[n][0])
                def _():
                    route(n).start()
        to_twin(slot).start()

    offset = lax.broadcasted_iota(jnp.int32, (TOK, 128), 0).astype(F32)

    def augmented(block, slot):
        word = block[slot, 4 * HD:].astype(F32)
        turned = pltpu.roll(word, 64, 1)
        start = jnp.where(lane16 < 64, word * 128.0 + turned, turned * 128.0 + word)
        bias = jnp.concatenate(
            [
                jnp.where(start[d:d + 1, :] + offset <= q_pos, 0.0, MASKED).astype(BF)
                for d in range(NZ)
            ],
            axis=0,
        )
        return jnp.concatenate([block[slot, 0:2 * HD], bias], axis=1)

    def keys_of(slot):
        return jnp.concatenate([augmented(mine, slot), augmented(theirs, slot)], axis=0)

    def values_of(slot):
        parts = [
            block[slot, at:at + HD] for block in (mine, theirs) for at in (2 * HD, 3 * HD)
        ]
        return jnp.concatenate(
            [jnp.concatenate(parts, axis=1), jnp.ones((TOK, KEYS), BF)], axis=0
        )

    def score(cc, keys, into, peak):
        scores = jnp.dot(keys, q_t[:, cc * 256:(cc + 1) * 256], preferred_element_type=F32)
        into[cc] = scores
        peak[cc] = jnp.max(scores, axis=0, keepdims=True)

    def absorb(cc, values, source, peak):
        old = top[cc]
        new = jnp.maximum(old, peak[cc])
        probs = jnp.exp2((source[cc] - new) * RATE).astype(BF)
        acc[cc] = acc[cc] * jnp.exp2((old - new) * RATE) + jnp.dot(
            values, probs, preferred_element_type=F32
        )
        top[cc] = new

    def step(slot, source, peak, into, into_peak):
        keys = keys_of(slot + 1)
        values = values_of(slot)
        for cc in range(4):
            score(cc, keys, into, into_peak)
            absorb(cc, values, source, peak)

    pass_on(0)
    wait_mine(1)
    pass_on(1)
    wait_theirs(0)
    keys = keys_of(0)
    for cc in range(4):
        score(cc, keys, even, peak_even)

    def pair(i, carry):
        slot = 2 * i
        wait_mine(slot + 2)
        pass_on(slot + 2)
        wait_theirs(slot + 1)
        step(slot, even, peak_even, odd, peak_odd)
        wait_mine(slot + 3)
        pass_on(slot + 3)
        wait_theirs(slot + 2)
        step(slot + 1, odd, peak_odd, even, peak_even)
        return carry

    lax.fori_loop(0, 7, pair, 0)
    wait_theirs(15)
    step(14, even, peak_even, odd, peak_odd)
    values = values_of(15)
    for cc in range(4):
        absorb(cc, values, odd, peak_odd)

    columns = pl.ds(pl.multiple_of(head * WIDTH, WIDTH), WIDTH)
    out_copies = []
    for j in (2, 1, 3, 0):
        cc = (head + j) % KVH
        done = (acc[cc, 0:HD] / acc[cc, HD:HD + 1]).T.astype(BF)
        for g in range(GROUP):
            out_stage[j, :, g * HD:(g + 1) * HD] = done[g * TOK:(g + 1) * TOK, :]
        if j == 0:
            out_copies.append(pltpu.make_async_copy(
                out_stage.at[j], out_ref.at[:, columns], o_send.at[j]
            ))
        else:
            to = device(x, y, (z // KVH) * KVH + cc, core)
            out_copies.append(remote(
                out_stage.at[j], out_ref.at[:, columns], o_send.at[j], o_recv.at[j], to
            ))
        out_copies[-1].start()
    for copy in line_copies:
        copy.wait_send()
    for n in range(len(ROUTES)):
        route(n).wait_send()
    for slot in range(16):
        to_twin(slot).wait_send()
    for j in (1, 2, 3):
        source = (head - j + KVH) % KVH
        place = out_ref.at[:, pl.ds(pl.multiple_of(source * WIDTH, WIDTH), WIDTH)]
        pltpu.make_async_copy(place, place, o_recv.at[j]).wait()
    for copy in out_copies[:3]:
        copy.wait_send()
    out_copies[3].wait()


def shards(queries, keys, values, order):
    dma = pltpu.SemaphoreType.DMA
    return pl.pallas_call(
        kernel,
        out_shape=jax.ShapeDtypeStruct((TOK, KVH * WIDTH), BF),
        in_specs=[pl.BlockSpec(memory_space=pl.ANY)] * 4,
        out_specs=pl.BlockSpec(memory_space=pltpu.VMEM),
        scratch_shapes=[
            pltpu.VMEM((16, BLOCK, HD), BF),
            pltpu.VMEM((16, BLOCK, HD), BF),
            pltpu.VMEM((KVH, 2, TOK, HD), BF),
            pltpu.VMEM((NZ, 2, TOK, HD), BF),
            pltpu.SMEM((TOK,), jnp.int32),
            pltpu.VMEM((1, 128), jnp.int32),
            pltpu.VMEM((NZ, 1, 128), jnp.int32),
            pltpu.VMEM((QTOK, WIDTH), BF),
            pltpu.VMEM((2 * HD, 1024), BF),
            pltpu.VMEM((4, KEYS, 256), F32),
            pltpu.VMEM((4, KEYS, 256), F32),
            pltpu.VMEM((4, 1, 256), F32),
            pltpu.VMEM((4, 1, 256), F32),
            pltpu.VMEM((4, HD + TOK, 256), F32),
            pltpu.VMEM((4, 1, 256), F32),
            pltpu.VMEM((4, TOK, WIDTH), BF),
            dma, dma, dma,
            dma((NZ - 1,)), dma, dma((NZ - 1,)), dma,
            dma((len(ROUTES),)), dma((16,)), dma((16,)), dma((16,)), dma((4,)), dma((4,)),
        ],
        compiler_params=pltpu.CompilerParams(
            collective_id=0, has_side_effects=True, vmem_limit_bytes=60 * 1024 * 1024
        ),
        cost_estimate=pl.CostEstimate(
            flops=4 * 1024 * 8192 * 128, bytes_accessed=1 << 20, transcendentals=1024 * 8192
        ),
    )(queries, keys, values, order)


def solution(mesh):
    return jax.shard_map(
        shards,
        mesh=mesh,
        in_specs=(
            P("row", None),
            P(("row", "col"), None),
            P(("row", "col"), None),
            P(("row", "col")),
        ),
        out_specs=P(("row", "col"), None),
        check_vma=False,
    )
```

time: 71.7 us -> 57.4 us (0.80)
  the two profiles are of different devices: /device:TPU:2 before, /device:TPU:1 now
where the time goes in v2:
time: 57.4 us; the launch traced here: 57.2 us
  Pallas kernels  55.5 us (97%)
  local copies, waits for them, and re-layouts  1.67 us (3%)
    pallas_call x1, Pallas kernels, shards(): pl.pallas_call(kernel, out_shape=jax.ShapeDtypeStruct((TOK, KVH * WIDTH),...  55.5 us
    unnamed x1, local copies, waits for them, and re-layouts  1.67 us

profile of v2, /device:TPU:1, one launch (start us, length us, event | category | flops | bytes accessed | tf_op | source)
XLA Modules:
  0.0 57.2 jit_solution(1001205644372786694)
XLA Ops:
  0.0 55.5 %shard_map.46 = bf16[16,8192]{1,0:T(8,128)(2,1)} custom-call(bf16[128,8192]{1,0:T(8,128)(2,1)} %q_hbm.1, bf16[16,512]{1,0:T(8,128)(2,1)} %k_hbm.1, bf16[16,512]{1,0:T(8,128)(2,1)} %v_hbm.1, s32[16]{0:T(128)} %order_hbm.1), custom_call_target="tpu_custom_call" | custom-call | flops 4294967296 | bytes 1048576 | tf_op jit(solution)/shard_map/pallas_call | solution.py:282
  55.5 1.7 %copy.6 = bf16[16,8192]{1,0:T(8,128)(2,1)} copy(bf16[16,8192]{1,0:T(8,128)(2,1)} %shard_map.46) | data formatting | bytes 524288

commit v3 on v2

--- a/solution.py
+++ b/solution.py
@@ -14,34 +14,49 @@
 NX, NY, NZ, NLO = 4, 4, 16, 8
 QTOK = 64
 WIDTH = GROUP * HD
-BLOCK = 2 * 2 * HD + TOK
-KEYS = 2 * NZ * TOK
+HALF = 8
+BKEYS = HALF * TOK
+BLOCK = BKEYS + HD + TOK
+KEYS = 4 * BKEYS
 BF = jnp.bfloat16
 F32 = jnp.float32
 MASKED = -1e30
 RATE = math.log2(math.e) / math.sqrt(HD)
 
 ORDER = [
-    (0, 0), (1, 0), (3, 0), (0, 1), (0, 3), (2, 0), (1, 1), (1, 3),
-    (3, 1), (3, 3), (0, 2), (2, 1), (2, 3), (1, 2), (3, 2), (2, 2),
+    (0, 0, 0), (1, 0, 0), (3, 0, 0), (0, 1, 0), (0, 3, 0), (0, 0, 1), (2, 0, 0), (1, 1, 0),
+    (3, 1, 0), (1, 3, 0), (3, 3, 0), (0, 2, 0), (1, 0, 1), (3, 0, 1), (0, 1, 1), (0, 3, 1),
+    (2, 1, 0), (2, 3, 0), (2, 0, 1), (1, 1, 1), (3, 1, 1), (1, 3, 1), (3, 3, 1), (1, 2, 0),
+    (3, 2, 0), (0, 2, 1), (2, 1, 1), (2, 3, 1), (1, 2, 1), (3, 2, 1), (2, 2, 0), (2, 2, 1),
 ]
+BLOCKS = len(ORDER)
 SLOT = {place: index for index, place in enumerate(ORDER)}
 STEP = {"A-": (1, 0), "A+": (-1, 0), "B-": (0, 1), "B+": (0, -1)}
-FORWARD = {
-    (0, 0): ["A-", "A+", "B-", "B+"],
-    (1, 0): ["A-", "B-", "B+"],
-    (3, 0): ["B-", "B+"],
-    (2, 0): ["B-", "B+"],
-    (0, 1): ["B-"],
-    (1, 1): ["B-"],
-    (2, 3): ["B+"],
-    (3, 3): ["B+"],
-}
+
+
+def onward(a, b, wave):
+    ways = []
+    if b == 0:
+        if a == 0:
+            ways += ["A-", "A+"]
+        if (a, wave) == (1, 0):
+            ways.append("A-")
+        if (a, wave) == (3, 1):
+            ways.append("A+")
+        ways += ["B-", "B+"]
+    if (b, wave) == (1, 0):
+        ways.append("B-")
+    if (b, wave) == (3, 1):
+        ways.append("B+")
+    return ways
+
+
 ROUTES = []
 for place in ORDER:
-    for way in FORWARD.get(place, []):
+    for way in onward(*place):
         da, db = STEP[way]
-        ROUTES.append((SLOT[place], way, SLOT[((place[0] + da) % 4, (place[1] + db) % 4)]))
+        there = ((place[0] + da) % 4, (place[1] + db) % 4, place[2])
+        ROUTES.append((SLOT[place], way, SLOT[there]))
 
 
 def kernel(
@@ -100,14 +115,15 @@
         )
 
     line_copies = []
-    for n, d in enumerate([8, 7, 9, 6, 10, 5, 11, 4, 12, 3, 13, 2, 14, 1, 15]):
-        at = NZ - d
-        line_copies.append(remote(
-            stage.at[(z + d) % KVH], landed.at[at], z_send.at[n], z_recv, line[d]
-        ))
-        line_copies.append(remote(
-            pos_own, pos_line.at[at], p_send.at[n], p_recv, line[d]
-        ))
+    for wave, ds in enumerate(([12, 13, 3, 14, 2, 15, 1], [8, 7, 9, 6, 10, 5, 11, 4])):
+        for d in ds:
+            at = wave * HALF + (NZ - d) % HALF
+            line_copies.append(remote(
+                stage.at[(z + d) % KVH], landed.at[at], z_send.at[d - 1], z_recv.at[wave], line[d]
+            ))
+            line_copies.append(remote(
+                pos_own, pos_line.at[at], p_send.at[d - 1], p_recv.at[wave], line[d]
+            ))
     for copy in line_copies:
         copy.start()
     landed[0] = stage[head]
@@ -127,72 +143,71 @@
     acc[...] = jnp.zeros_like(acc)
     top[...] = jnp.full_like(top, MASKED)
 
-    pltpu.make_async_copy(pos_line.at[pl.ds(1, NZ - 1)], pos_line.at[pl.ds(1, NZ - 1)], p_recv).wait()
-    starts = jnp.concatenate([pos_line[d] for d in range(NZ)], axis=0)
     lane16 = lax.broadcasted_iota(jnp.int32, (TOK, 128), 1)
-    mine[0, 4 * HD:] = jnp.where(lane16 < 64, starts // 128, starts % 128).astype(F32).astype(BF)
+
+    def collect(wave):
+        first = 1 - wave
+        got = pos_line.at[pl.ds(wave * HALF + first, HALF - first)]
+        pltpu.make_async_copy(got, got, p_recv.at[wave]).wait()
+        got = landed.at[pl.ds(wave * HALF + first, HALF - first)]
+        pltpu.make_async_copy(got, got, z_recv.at[wave]).wait()
+        slot = SLOT[(0, 0, wave)]
+        places = [wave * HALF + d for d in range(HALF)]
+        starts = jnp.concatenate([pos_line[d] for d in places * 2], axis=0)
+        mine[slot, BKEYS + HD:] = jnp.where(
+            lane16 < 64, starts // 128, starts % 128
+        ).astype(F32).astype(BF)
+        for d in range(HALF):
+            mine[slot, d * TOK:(d + 1) * TOK] = landed[wave * HALF + d, 0]
+        mine[slot, BKEYS:BKEYS + HD] = jnp.concatenate([landed[d, 1] for d in places], axis=0).T
+
+    def route(n):
+        slot, way, there = ROUTES[n]
+        return remote(mine.at[slot], mine.at[there], f_send.at[n], m_recv.at[there], plane[way])
+
+    def to_twin(slot):
+        return remote(mine.at[slot], theirs.at[slot], c_send.at[slot], t_recv.at[slot], twin)
+
+    def wait_mine(slot):
+        pltpu.make_async_copy(mine.at[slot], mine.at[slot], m_recv.at[slot]).wait()
+
+    def wait_theirs(slot):
+        pltpu.make_async_copy(theirs.at[slot], theirs.at[slot], t_recv.at[slot]).wait()
+
+    def pass_on(slot):
+        for n in range(len(ROUTES)):
+            if ROUTES[n][0] == slot:
+                route(n).start()
+        to_twin(slot).start()
+
+    collect(0)
+    pass_on(0)
+
     lane1 = lax.broadcasted_iota(jnp.int32, (1, 128), 1)
     q_pos = jnp.zeros((1, 128), jnp.int32)
     for cc in range(4):
         q_pos = jnp.where(
-            lane1 // TOK == cc, pos_line[(cc - head + NZ) % NZ] + lane1 % TOK, q_pos
-        )
-    q_pos = q_pos.astype(F32)
-
-    rest = landed.at[pl.ds(1, NZ - 1)]
-    pltpu.make_async_copy(rest, rest, z_recv).wait()
-    for d in range(NZ):
-        mine[0, d * TOK:(d + 1) * TOK] = landed[d, 0]
-    for part in range(2):
-        values = jnp.concatenate([landed[part * 8 + d, 1] for d in range(8)], axis=0)
-        mine[0, (2 + part) * HD:(3 + part) * HD] = values.T
-
-    def route(n):
-        slot, way, there = ROUTES[n]
-        return remote(mine.at[slot], mine.at[there], f_send.at[n], m_recv.at[there], plane[way])
-
-    def to_twin(slot):
-        return remote(mine.at[slot], theirs.at[slot], c_send.at[slot], t_recv.at[slot], twin)
-
-    def wait_mine(slot):
-        pltpu.make_async_copy(mine.at[slot], mine.at[slot], m_recv.at[slot]).wait()
-
-    def wait_theirs(slot):
-        pltpu.make_async_copy(theirs.at[slot], theirs.at[slot], t_recv.at[slot]).wait()
-
-    def pass_on(slot):
-        for n in range(len(ROUTES)):
-            if isinstance(slot, int):
-                if ROUTES[n][0] == slot:
-                    route(n).start()
-            elif ROUTES[n][0] > 1:
-                @pl.when(slot == ROUTES[n][0])
-                def _():
-                    route(n).start()
-        to_twin(slot).start()
-
-    offset = lax.broadcasted_iota(jnp.int32, (TOK, 128), 0).astype(F32)
+            lane1 // TOK == cc, pos_line[(cc - head + HALF) % HALF] + lane1 % TOK, q_pos
+        )
+    limit = (q_pos - lax.broadcasted_iota(jnp.int32, (TOK, 128), 0)).astype(F32)
 
     def augmented(block, slot):
-        word = block[slot, 4 * HD:].astype(F32)
+        word = block[slot, BKEYS + HD:].astype(F32)
         turned = pltpu.roll(word, 64, 1)
         start = jnp.where(lane16 < 64, word * 128.0 + turned, turned * 128.0 + word)
         bias = jnp.concatenate(
-            [
-                jnp.where(start[d:d + 1, :] + offset <= q_pos, 0.0, MASKED).astype(BF)
-                for d in range(NZ)
-            ],
+            [jnp.where(start[d:d + 1, :] <= limit, 0.0, MASKED).astype(BF) for d in range(HALF)],
             axis=0,
         )
-        return jnp.concatenate([block[slot, 0:2 * HD], bias], axis=1)
-
-    def keys_of(slot):
-        return jnp.concatenate([augmented(mine, slot), augmented(theirs, slot)], axis=0)
-
-    def values_of(slot):
-        parts = [
-            block[slot, at:at + HD] for block in (mine, theirs) for at in (2 * HD, 3 * HD)
-        ]
+        return jnp.concatenate([block[slot, 0:BKEYS], bias], axis=1)
+
+    def keys_of(s):
+        return jnp.concatenate(
+            [augmented(block, 2 * s + k) for block in (mine, theirs) for k in (0, 1)], axis=0
+        )
+
+    def values_of(s):
+        parts = [block[2 * s + k, BKEYS:BKEYS + HD] for block in (mine, theirs) for k in (0, 1)]
         return jnp.concatenate(
             [jnp.concatenate(parts, axis=1), jnp.ones((TOK, KEYS), BF)], axis=0
         )
@@ -211,36 +226,51 @@
         )
         top[cc] = new
 
-    def step(slot, source, peak, into, into_peak):
-        keys = keys_of(slot + 1)
-        values = values_of(slot)
+    def step(s, source, peak, into, into_peak):
+        keys = keys_of(s + 1)
+        values = values_of(s)
         for cc in range(4):
             score(cc, keys, into, into_peak)
             absorb(cc, values, source, peak)
 
-    pass_on(0)
     wait_mine(1)
     pass_on(1)
     wait_theirs(0)
+    wait_theirs(1)
     keys = keys_of(0)
     for cc in range(4):
         score(cc, keys, even, peak_even)
+    for slot in (2, 3):
+        wait_mine(slot)
+        pass_on(slot)
+    wait_theirs(2)
+    wait_theirs(3)
+    step(0, even, peak_even, odd, peak_odd)
+    wait_mine(4)
+    pass_on(4)
+    collect(1)
+    pass_on(5)
 
     def pair(i, carry):
-        slot = 2 * i
-        wait_mine(slot + 2)
-        pass_on(slot + 2)
-        wait_theirs(slot + 1)
-        step(slot, even, peak_even, odd, peak_odd)
-        wait_mine(slot + 3)
-        pass_on(slot + 3)
-        wait_theirs(slot + 2)
-        step(slot + 1, odd, peak_odd, even, peak_even)
+        for k in range(2):
+            s = 2 * i + 1 + k
+            for v in range(7):
+                first = 4 * v + 6 + 2 * k
+                if first < BLOCKS:
+                    @pl.when(i == v)
+                    def _():
+                        for slot in (first, first + 1):
+                            wait_mine(slot)
+                            pass_on(slot)
+            wait_theirs(2 * s + 2)
+            wait_theirs(2 * s + 3)
+            if k == 0:
+                step(s, odd, peak_odd, even, peak_even)
+            else:
+                step(s, even, peak_even, odd, peak_odd)
         return carry
 
     lax.fori_loop(0, 7, pair, 0)
-    wait_theirs(15)
-    step(14, even, peak_even, odd, peak_odd)
     values = values_of(15)
     for cc in range(4):
         absorb(cc, values, odd, peak_odd)
@@ -266,7 +296,7 @@
         copy.wait_send()
     for n in range(len(ROUTES)):
         route(n).wait_send()
-    for slot in range(16):
+    for slot in range(BLOCKS):
         to_twin(slot).wait_send()
     for j in (1, 2, 3):
         source = (head - j + KVH) % KVH
@@ -283,10 +313,10 @@
         kernel,
         out_shape=jax.ShapeDtypeStruct((TOK, KVH * WIDTH), BF),
         in_specs=[pl.BlockSpec(memory_space=pl.ANY)] * 4,
-        out_specs=pl.BlockSpec(memory_space=pltpu.VMEM),
+        out_specs=pl.BlockSpec(memory_space=pl.ANY),
         scratch_shapes=[
-            pltpu.VMEM((16, BLOCK, HD), BF),
-            pltpu.VMEM((16, BLOCK, HD), BF),
+            pltpu.VMEM((BLOCKS, BLOCK, HD), BF),
+            pltpu.VMEM((BLOCKS, BLOCK, HD), BF),
             pltpu.VMEM((KVH, 2, TOK, HD), BF),
             pltpu.VMEM((NZ, 2, TOK, HD), BF),
             pltpu.SMEM((TOK,), jnp.int32),
@@ -302,8 +332,9 @@
             pltpu.VMEM((4, 1, 256), F32),
             pltpu.VMEM((4, TOK, WIDTH), BF),
             dma, dma, dma,
-            dma((NZ - 1,)), dma, dma((NZ - 1,)), dma,
-            dma((len(ROUTES),)), dma((16,)), dma((16,)), dma((16,)), dma((4,)), dma((4,)),
+            dma((NZ - 1,)), dma((2,)), dma((NZ - 1,)), dma((2,)),
+            dma((len(ROUTES),)), dma((BLOCKS,)), dma((BLOCKS,)), dma((BLOCKS,)),
+            dma((4,)), dma((4,)),
         ],
         compiler_params=pltpu.CompilerParams(
             collective_id=0, has_side_effects=True, vmem_limit_bytes=60 * 1024 * 1024

time: 57.4 us -> 58.4 us (1.017)
  Pallas kernels: 55.5 us -> 56.6 us
    pallas_call x1, Pallas kernels: 55.5 us -> 56.6 us  [shards(): pl.pallas_call(kernel, out_shape=jax.ShapeDtypeStruct((TOK, KVH * WIDTH),...]
where the time goes in v3:
time: 58.4 us; the launch traced here: 58.3 us
  Pallas kernels  56.6 us (97%)
  local copies, waits for them, and re-layouts  1.67 us (3%)
    pallas_call x1, Pallas kernels, shards(): pl.pallas_call(kernel, out_shape=jax.ShapeDtypeStruct((TOK, KVH * WIDTH),...  56.6 us
    unnamed x1, local copies, waits for them, and re-layouts  1.67 us

profile of v3, /device:TPU:1, one launch (start us, length us, event | category | flops | bytes accessed | tf_op | source)
XLA Modules:
  0.0 58.3 jit_solution(10436031821452277021)
XLA Ops:
  0.0 56.6 %shard_map.46 = bf16[16,8192]{1,0:T(8,128)(2,1)} custom-call(bf16[128,8192]{1,0:T(8,128)(2,1)} %q_hbm.1, bf16[16,512]{1,0:T(8,128)(2,1)} %k_hbm.1, bf16[16,512]{1,0:T(8,128)(2,1)} %v_hbm.1, s32[16]{0:T(128)} %order_hbm.1), custom_call_target="tpu_custom_call" | custom-call | flops 4294967296 | bytes 1048576 | tf_op jit(solution)/shard_map/pallas_call | solution.py:312
  56.6 1.7 %copy.6 = bf16[16,8192]{1,0:T(8,128)(2,1)} copy(bf16[16,8192]{1,0:T(8,128)(2,1)} %shard_map.46) | data formatting | bytes 524288
